TPU v7x, 32 devices: a whole 2x2x4 slice. The times are simulated.
32 devices in a mesh: wide: 16 (over z, y, x), deep: 2 (over core).
Axes of the slice: x: 2, y: 2, z: 4, core: 2. Of those that a mesh axis runs over, the one named last changes fastest.
Arguments:
- rhs_local: float32 [256, 32, 128], P('wide', 'deep'), may hold values from -6 to 6
- metric: float32 [3, 256, 32, 128], P(None, 'wide', 'deep'), may hold values from 0.005 to 0.05
- helm: float32 [256, 32, 128], P('wide', 'deep'), may hold values from 0.5 to 4
- columns: int32 [16, 4, 4, 8], P('wide', 'deep'), may hold values from 0 to 23
- live_blocks: int32 [16, 4, 4], P('wide', 'deep'), may hold values from 1 to 8
- block_values: float32 [16, 4, 4, 512], P('wide', 'deep'), may hold values from -0.0234375 to 0.0234375
Outputs:
- smoothed: float32 [256, 32, 128], P('wide', 'deep')
- coarse_product: float32 [16, 4, 32], P('wide', 'deep')
All inputs are finite; a program needn't handle non-finite values.
Results may differ from a plain program's by a relative error of at most 0.00013.
Values sent between devices are 32-bit elements; how exact they have to be, the bound alone decides.
A program may use at most 64 MiB of HBM per device.

v0:
```python
import jax
import jax.numpy as jnp
import numpy as np
from jax import lax
from jax.sharding import PartitionSpec as P

NP = 8
K = 8
BS = 8


upper_bound = 6.0
lower_bound = 0.6
highest = lax.Precision.HIGHEST


def extended(block, sides, width):
    for axis, dim in sides:
        count = lax.axis_size(axis)
        forward = [(i, i + 1) for i in range(count - 1)]
        forward.append((count - 1, 0))
        backward = [(target, source) for source, target in forward]
        low = lax.ppermute(
            lax.slice_in_dim(block, block.shape[dim] - width, None, axis=dim), axis, forward
        )
        high = lax.ppermute(lax.slice_in_dim(block, 0, width, axis=dim), axis, backward)
        block = jnp.concatenate([low, block, high], axis=dim)
    return block


def gll_tables(count):
    order = count - 1
    nodes = np.cos(np.pi * np.arange(count) / order)
    legendre = np.zeros((count, count))
    for sweep in range(101):
        legendre[:, 0] = 1.0
        legendre[:, 1] = nodes
        for degree in range(2, count):
            legendre[:, degree] = (
                (2 * degree - 1) * nodes * legendre[:, degree - 1]
                - (degree - 1) * legendre[:, degree - 2]
            ) / degree
        if sweep < 100:
            nodes = nodes - (nodes * legendre[:, order] - legendre[:, order - 1]) / (
                count * legendre[:, order]
            )
    nodes = nodes[::-1].copy()
    values = legendre[::-1, order].copy()
    identity_table = np.eye(count)
    spacing = nodes[:, None] - nodes[None, :] + identity_table
    derivative = values[:, None] / values[None, :] / spacing
    derivative = derivative * (1.0 - identity_table)
    derivative[0, 0] = -order * (order + 1) / 4.0
    derivative[-1, -1] = order * (order + 1) / 4.0
    linear = np.stack([(1.0 - nodes) / 2.0, (1.0 + nodes) / 2.0], axis=1)
    return (jnp.asarray(derivative, jnp.float32), jnp.asarray(linear, jnp.float32))


def block_extent():
    return 128


def repeat_table(small, copies):
    return jnp.kron(jnp.eye(copies, dtype=jnp.float32), small)


def contract(field, table, axis):
    if axis == 0:
        return jnp.einsum("mi,iyz->myz", table, field, precision=highest)
    if axis == 1:
        return jnp.einsum("mj,xjz->xmz", table, field, precision=highest)
    shape = field.shape
    blocked = table.shape[1]
    grid = field.reshape(shape[0], shape[1], shape[2] // blocked, blocked)
    result = jnp.einsum("mk,xynk->xynm", table, grid, precision=highest)
    return result.reshape(shape[0], shape[1], -1)


def pair_sum(field, axis, count, wrap):

    def pick(start):
        index = [slice(None), slice(None), slice(None)]
        index[axis] = slice(start, None, count)
        return tuple(index)

    first = field[pick(0)]
    last = field[pick(count - 1)]
    if wrap:
        shared = last + jnp.roll(first, -1, axis=axis)
        new_last = shared
        new_first = jnp.roll(shared, 1, axis=axis)
    else:
        length = last.shape[axis]
        shared = lax.slice_in_dim(last, 0, length - 1, axis=axis) + lax.slice_in_dim(
            first, 1, length, axis=axis
        )
        new_last = jnp.concatenate(
            [shared, lax.slice_in_dim(last, length - 1, length, axis=axis)], axis=axis
        )
        new_first = jnp.concatenate([lax.slice_in_dim(first, 0, 1, axis=axis), shared], axis=axis)
    return field.at[pick(count - 1)].set(new_last).at[pick(0)].set(new_first)


def assemble(field, count):
    field = pair_sum(field, 0, count, False)
    field = pair_sum(field, 1, count, False)
    field = pair_sum(field, 2, count, True)
    padded = extended(field, (("wide", 0),), 1)
    field = field.at[0].add(padded[0]).at[-1].add(padded[-1])
    padded = extended(field, (("deep", 1),), 1)
    field = field.at[:, 0].add(padded[:, 0]).at[:, -1].add(padded[:, -1])
    return field


def apply_operator(field, metric, helm, tables):
    total = helm * field
    for axis in range(3):
        slope = contract(field, tables[axis], axis)
        total = total + contract(metric[axis] * slope, tables[axis].T, axis)
    return total


def chebyshev(solution, rhs_local, metric, helm, tables, inverse, from_zero):
    centre = (upper_bound + lower_bound) / 2.0
    half_width = (upper_bound - lower_bound) / 2.0
    aspect = centre / half_width
    weight_prev = 1.0 / aspect
    if from_zero:
        residual = assemble(rhs_local, NP)
    else:
        residual = assemble(rhs_local - apply_operator(solution, metric, helm, tables), NP)
    update = inverse * residual / centre
    solution = solution + update
    residual = assemble(rhs_local - apply_operator(solution, metric, helm, tables), NP)
    weight_next = 1.0 / (2.0 * aspect - weight_prev)
    update = (
        weight_next * weight_prev * update + 2.0 * weight_next / half_width * inverse * residual
    )
    solution = solution + update
    return solution


def local(rhs_local, metric, helm, columns, live_blocks, block_values):
    derivative, linear = gll_tables(NP)
    shape = rhs_local.shape
    copies = (shape[0] // NP, shape[1] // NP, block_extent() // NP)
    tables = tuple((repeat_table(derivative, copies[axis]) for axis in range(3)))
    square_tables = tuple(
        (repeat_table(derivative * derivative, copies[axis]) for axis in range(3))
    )
    down_tables = tuple((repeat_table(linear.T, copies[axis]) for axis in range(3)))
    up_tables = tuple((repeat_table(linear, copies[axis]) for axis in range(3)))
    diagonal = helm
    for axis in range(3):
        diagonal = diagonal + contract(metric[axis], square_tables[axis].T, axis)
    inverse = 1.0 / assemble(diagonal, NP)
    first = chebyshev(jnp.zeros_like(rhs_local), rhs_local, metric, helm, tables, inverse, True)
    local_res = rhs_local - apply_operator(first, metric, helm, tables)
    corners = local_res
    for axis in range(3):
        corners = contract(corners, down_tables[axis], axis)
    assembled = assemble(corners, 2)
    vertices = assembled[::2, ::2, ::2]
    layers = columns.shape[0]
    owned = lax.all_to_all(
        jnp.transpose(vertices, (2, 1, 0)), "wide", split_axis=0, concat_axis=2, tiled=True
    )
    frame = extended(owned, (("wide", 0),), layers)
    span = frame.shape[2]
    frame_rows = frame.reshape(-1, BS)
    picked = jnp.take(frame_rows, columns.reshape(-1), axis=0).reshape(columns.shape + (BS,))
    live = (
        jnp.arange(K, dtype=jnp.int32)[None, None, None, :] < live_blocks[:, :, :, None]
    ).astype(jnp.float32)
    values = block_values.reshape(columns.shape + (BS, BS))
    product = jnp.einsum("zyxkij,zyxkj,zyxk->zyxi", values, picked, live, precision=highest)
    coarse_product = product.reshape(layers, frame.shape[1], span)
    returned = lax.all_to_all(coarse_product, "wide", split_axis=2, concat_axis=0, tiled=True)
    coarse_vertices = jnp.transpose(returned, (2, 1, 0))
    holder = jnp.zeros(corners.shape, jnp.float32).at[::2, ::2, ::2].set(coarse_vertices)
    correction = assemble(holder, 2)
    for axis in range(3):
        correction = contract(correction, up_tables[axis], axis)
    second = first + correction
    smoothed = chebyshev(second, rhs_local, metric, helm, tables, inverse, False)
    return (smoothed, coarse_product)


def solution(mesh):
    placed = (
        P("wide", "deep", None),
        P(None, "wide", "deep", None),
        P("wide", "deep", None),
        P("wide", "deep", None, None),
        P("wide", "deep", None),
        P("wide", "deep", None, None),
    )
    return jax.shard_map(
        local,
        mesh=mesh,
        in_specs=placed,
        out_specs=(P("wide", "deep", None), P("wide", "deep", None)),
        check_vma=False,
    )
```

profile of v0, /device:TPU:0, one launch (start us, length us, event | category | flops | bytes accessed | tf_op | source)
XLA Modules:
  0.0 204.3 jit_solution(12693977727114605595)
XLA Ops:
  10.2 3.0 %collective-permute-start.4 = (f32[1,16,128]{2,0,1:T(1,128)S(1)}, f32[1,16,128]{2,0,1:T(1,128)S(1)}, u32[]{:S(2)}, u32[]{:S(2)}) collective-permute-start(f32[1,16,128]{2,0,1:T(1,128)S(1)} %slice.1290), channel_id=1, source_target_pairs={{0,2},{2,4},{4,6},{6,8},{8,10},{10,12},{12,14},{14,16},{16,18},{18... | collective-permute-start | bytes 24584 | tf_op jit(solution)/shard_map/ppermute | solution.py:23
  26.0 1.5 collective-permute-start
  29.9 4.2 %collective-permute-start.5 = (f32[1,16,128]{2,0,1:T(1,128)S(1)}, f32[1,16,128]{2,0,1:T(1,128)S(1)}, u32[]{:S(2)}, u32[]{:S(2)}) collective-permute-start(f32[1,16,128]{2,0,1:T(1,128)S(1)} %get-tuple-element.364), channel_id=1, source_target_pairs={{2,0},{4,2},{6,4},{8,6},{10,8},{12,10},{14,12},{16,14},{18,16},{20... | collective-permute-start | bytes 24584 | tf_op jit(solution)/shard_map/ppermute | solution.py:26
  35.6 2.3 %collective-permute-done.1 = f32[1,16,128]{2,0,1:T(1,128)S(1)} collective-permute-done((f32[1,16,128]{2,0,1:T(1,128)S(1)}, f32[1,16,128]{2,0,1:T(1,128)S(1)}, u32[]{:S(2)}, u32[]{:S(2)}) %collective-permute-start.1) | collective-permute-done | bytes 8224 | tf_op jit(solution)/shard_map/ppermute | solution.py:26
  51.2 7.2 %collective-permute-done.8 = f32[1,16,128]{2,0,1:T(1,128)S(1)} collective-permute-done((f32[1,16,128]{2,0,1:T(1,128)S(1)}, f32[1,16,128]{2,0,1:T(1,128)S(1)}, u32[]{:S(2)}, u32[]{:S(2)}) %collective-permute-start.8) | collective-permute-done | bytes 8224 | tf_op jit(solution)/shard_map/ppermute | solution.py:23
  59.6 2.6 %collective-permute-done.9 = f32[1,16,128]{2,0,1:T(1,128)S(1)} collective-permute-done((f32[1,16,128]{2,0,1:T(1,128)S(1)}, f32[1,16,128]{2,0,1:T(1,128)S(1)}, u32[]{:S(2)}, u32[]{:S(2)}) %collective-permute-start.9) | collective-permute-done | bytes 8224 | tf_op jit(solution)/shard_map/ppermute | solution.py:26
  72.6 7.3 %collective-permute-done.12 = f32[1,4,32]{1,0,2:T(1,128)S(1)} collective-permute-done((f32[1,4,32]{1,0,2:T(1,128)S(1)}, f32[1,4,32]{1,0,2:T(1,128)S(1)}, u32[]{:S(2)}, u32[]{:S(2)}) %collective-permute-start.12) | collective-permute-done | bytes 544 | tf_op jit(solution)/shard_map/ppermute | solution.py:23
  81.1 2.6 %collective-permute-done.13 = f32[1,4,32]{1,0,2:T(1,128)S(1)} collective-permute-done((f32[1,4,32]{1,0,2:T(1,128)S(1)}, f32[1,4,32]{1,0,2:T(1,128)S(1)}, u32[]{:S(2)}, u32[]{:S(2)}) %collective-permute-start.13) | collective-permute-done | bytes 544 | tf_op jit(solution)/shard_map/ppermute | solution.py:26
  86.7 2.4 %scatter-add.119 = f32[4,4,32]{1,0,2:T(4,128)S(1)} dynamic-update-slice(f32[4,4,32]{1,0,2:T(4,128)S(1)} %scatter-add.116, f32[4,1,32]{1,0,2:T(4,128)S(1)} %slice_add_fusion.1, s32[]{:T(128)} %constant.639.clone.1, s32[]{:T(128)} %constant.649.clone.1, s32[]{:T(128)} %constant.639.clone.1) | dynamic-update-slice | bytes 1028 | tf_op jit(solution)/shard_map/scatter-add | solution.py:111
  89.2 5.2 %slice.1181 = f32[2,2,16]{1,0,2:T(2,128)} slice(f32[4,4,32]{1,0,2:T(4,128)S(1)} %scatter-add.119), slice={[0:4:2], [0:4:2], [0:32:2]} | slice | bytes 512 | tf_op jit(solution)/shard_map/slice | solution.py:163
  94.4 6.0 %all-to-all-start = ((f32[16,2,2]{1,2,0:T(2,128)}), f32[16,2,2]{1,2,0:T(2,128)S(1)}, u32[]{:S(2)}, u32[]{:S(2)}) async-start(f32[16,2,2]{1,2,0:T(2,128)} %bitcast.39), calls=%async_computation | async-start | bytes 32768 | tf_op jit(solution)/shard_map/all_to_all | solution.py:165
  100.4 7.3 %all-to-all-done = f32[16,2,2]{1,2,0:T(2,128)S(1)} async-done(((f32[16,2,2]{1,2,0:T(2,128)}), f32[16,2,2]{1,2,0:T(2,128)S(1)}, u32[]{:S(2)}, u32[]{:S(2)}) %all-to-all-start) | async-done | bytes 288 | tf_op jit(solution)/shard_map/all_to_all | solution.py:165
  110.0 1.4 collective-permute-done.17
  111.4 4.3 %collective-permute-done.16 = f32[1,2,32]{2,1,0:T(2,128)S(1)} collective-permute-done((f32[1,2,32]{2,1,0:T(2,128)S(1)}, f32[1,2,32]{2,1,0:T(2,128)S(1)}, u32[]{:S(2)}, u32[]{:S(2)}) %collective-permute-start.16) | collective-permute-done | bytes 288 | tf_op jit(solution)/shard_map/ppermute | solution.py:23
  117.9 3.7 %all-to-all-start.1 = ((f32[1,2,32]{1,0,2:T(1,128)}), f32[1,2,32]{1,0,2:T(1,128)S(1)}, u32[]{:S(2)}, u32[]{:S(2)}) async-start(f32[1,2,32]{1,0,2:T(1,128)} %copy.253), calls=%async_computation.1 | async-start | bytes 32768 | tf_op jit(solution)/shard_map/all_to_all | solution.py:178
  121.7 6.9 %all-to-all-done.1 = f32[1,2,32]{1,0,2:T(1,128)S(1)} async-done(((f32[1,2,32]{1,0,2:T(1,128)}), f32[1,2,32]{1,0,2:T(1,128)S(1)}, u32[]{:S(2)}, u32[]{:S(2)}) %all-to-all-start.1) | async-done | bytes 288 | tf_op jit(solution)/shard_map/all_to_all | solution.py:178
  129.0 4.4 %scatter_fusion.24 = f32[4,4,32]{2,1,0:T(4,128)S(1)} fusion(f32[4,4,32]{2,1,0:T(4,128)S(1)} %broadcast_in_dim.55, s32[64]{0:T(128)S(1)} %reshape.1259, f32[64]{0:T(128)S(1)} %reshape.1261), kind=kCustom, calls=%fused_computation.25 | custom fusion | bytes 1536 | tf_op jit(solution)/shard_map/scatter | solution.py:180
  139.7 6.7 %collective-permute-done.18 = f32[1,4,32]{1,0,2:T(1,128)S(1)} collective-permute-done((f32[1,4,32]{1,0,2:T(1,128)S(1)}, f32[1,4,32]{1,0,2:T(1,128)S(1)}, u32[]{:S(2)}, u32[]{:S(2)}) %collective-permute-start.18) | collective-permute-done | bytes 544 | tf_op jit(solution)/shard_map/ppermute | solution.py:23
  146.6 3.6 %collective-permute-done.19 = f32[1,4,32]{1,0,2:T(1,128)S(1)} collective-permute-done((f32[1,4,32]{1,0,2:T(1,128)S(1)}, f32[1,4,32]{1,0,2:T(1,128)S(1)}, u32[]{:S(2)}, u32[]{:S(2)}) %collective-permute-start.19) | collective-permute-done | bytes 544 | tf_op jit(solution)/shard_map/ppermute | solution.py:26
  153.2 2.4 %scatter-add.125 = f32[4,4,32]{1,0,2:T(4,128)S(1)} dynamic-update-slice(f32[4,4,32]{1,0,2:T(4,128)S(1)} %scatter-add.124, f32[4,1,32]{1,0,2:T(4,128)S(1)} %slice_add_fusion, s32[]{:T(128)} %constant.639.clone.1, s32[]{:T(128)} %constant.649.clone.1, s32[]{:T(128)} %constant.639.clone.1) | dynamic-update-slice | bytes 1028 | tf_op jit(solution)/shard_map/scatter-add | solution.py:111
  166.4 7.2 %collective-permute-done.22 = f32[1,16,128]{2,0,1:T(1,128)S(1)} collective-permute-done((f32[1,16,128]{2,0,1:T(1,128)S(1)}, f32[1,16,128]{2,0,1:T(1,128)S(1)}, u32[]{:S(2)}, u32[]{:S(2)}) %collective-permute-start.22) | collective-permute-done | bytes 8224 | tf_op jit(solution)/shard_map/ppermute | solution.py:23
  173.8 3.6 %collective-permute-done.23 = f32[1,16,128]{2,0,1:T(1,128)S(1)} collective-permute-done((f32[1,16,128]{2,0,1:T(1,128)S(1)}, f32[1,16,128]{2,0,1:T(1,128)S(1)}, u32[]{:S(2)}, u32[]{:S(2)}) %collective-permute-start.23) | collective-permute-done | bytes 8224 | tf_op jit(solution)/shard_map/ppermute | solution.py:26
  190.1 7.2 %collective-permute-done.26 = f32[1,16,128]{2,0,1:T(1,128)S(1)} collective-permute-done((f32[1,16,128]{2,0,1:T(1,128)S(1)}, f32[1,16,128]{2,0,1:T(1,128)S(1)}, u32[]{:S(2)}, u32[]{:S(2)}) %collective-permute-start.26) | collective-permute-done | bytes 8224 | tf_op jit(solution)/shard_map/ppermute | solution.py:23
  197.5 3.6 %collective-permute-done.27 = f32[1,16,128]{2,0,1:T(1,128)S(1)} collective-permute-done((f32[1,16,128]{2,0,1:T(1,128)S(1)}, f32[1,16,128]{2,0,1:T(1,128)S(1)}, u32[]{:S(2)}, u32[]{:S(2)}) %collective-permute-start.27) | collective-permute-done | bytes 8224 | tf_op jit(solution)/shard_map/ppermute | solution.py:26
  (420 shorter events, 94.8 us)
Async XLA Ops:
  10.2 19.7 %collective-permute-start.4 = (f32[1,16,128]{2,0,1:T(1,128)S(1)}, f32[1,16,128]{2,0,1:T(1,128)S(1)}, u32[]{:S(2)}, u32[]{:S(2)}) collective-permute-start(f32[1,16,128]{2,0,1:T(1,128)S(1)} %slice.1290), channel_id=1, source_target_pairs={{0,2},{2,4},{4,6},{6,8},{8,10},{10,12},{12,14},{14,16},{16,18},{18... | collective-permute-start | bytes 24584 | tf_op jit(solution)/shard_map/ppermute | solution.py:23
  26.0 8.1 %collective-permute-start = (f32[1,16,128]{2,0,1:T(1,128)S(1)}, f32[1,16,128]{2,0,1:T(1,128)S(1)}, u32[]{:S(2)}, u32[]{:S(2)}) collective-permute-start(f32[1,16,128]{2,0,1:T(1,128)S(1)} %slice.1272), channel_id=1, source_target_pairs={{0,2},{2,4},{4,6},{6,8},{8,10},{10,12},{12,14},{14,16},{16,18},{18... | collective-permute-start | bytes 24584 | tf_op jit(solution)/shard_map/ppermute | solution.py:23
  29.9 5.5 %collective-permute-start.5 = (f32[1,16,128]{2,0,1:T(1,128)S(1)}, f32[1,16,128]{2,0,1:T(1,128)S(1)}, u32[]{:S(2)}, u32[]{:S(2)}) collective-permute-start(f32[1,16,128]{2,0,1:T(1,128)S(1)} %get-tuple-element.364), channel_id=1, source_target_pairs={{2,0},{4,2},{6,4},{8,6},{10,8},{12,10},{14,12},{16,14},{18,16},{20... | collective-permute-start | bytes 24584 | tf_op jit(solution)/shard_map/ppermute | solution.py:26
  34.2 3.7 %collective-permute-start.1 = (f32[1,16,128]{2,0,1:T(1,128)S(1)}, f32[1,16,128]{2,0,1:T(1,128)S(1)}, u32[]{:S(2)}, u32[]{:S(2)}) collective-permute-start(f32[1,16,128]{2,0,1:T(1,128)S(1)} %get-tuple-element.360), channel_id=1, source_target_pairs={{2,0},{4,2},{6,4},{8,6},{10,8},{12,10},{14,12},{16,14},{18,16},{20... | collective-permute-start | bytes 24584 | tf_op jit(solution)/shard_map/ppermute | solution.py:26
  35.5 2.7 %collective-permute-start.6 = (f32[16,1,128]{2,0,1:T(8,128)S(1)}, f32[16,1,128]{2,0,1:T(8,128)S(1)}, u32[]{:S(2)}, u32[]{:S(2)}) collective-permute-start(f32[16,1,128]{2,0,1:T(8,128)S(1)} %slice.1293), channel_id=1, source_target_pairs={{0,1},{1,0},{2,3},{3,2},{4,5},{5,4},{6,7},{7,6},{8,9},{9,8},{10,11... | collective-permute-start | bytes 24584 | tf_op jit(solution)/shard_map/ppermute | solution.py:23
  38.3 1.3 collective-permute-start.7
  51.1 7.3 %collective-permute-start.8 = (f32[1,16,128]{2,0,1:T(1,128)S(1)}, f32[1,16,128]{2,0,1:T(1,128)S(1)}, u32[]{:S(2)}, u32[]{:S(2)}) collective-permute-start(f32[1,16,128]{2,0,1:T(1,128)S(1)} %slice.1308), channel_id=1, source_target_pairs={{0,2},{2,4},{4,6},{6,8},{8,10},{10,12},{12,14},{14,16},{16,18},{18... | collective-permute-start | bytes 24584 | tf_op jit(solution)/shard_map/ppermute | solution.py:23
  58.4 3.7 %collective-permute-start.9 = (f32[1,16,128]{2,0,1:T(1,128)S(1)}, f32[1,16,128]{2,0,1:T(1,128)S(1)}, u32[]{:S(2)}, u32[]{:S(2)}) collective-permute-start(f32[1,16,128]{2,0,1:T(1,128)S(1)} %get-tuple-element.356), channel_id=1, source_target_pairs={{2,0},{4,2},{6,4},{8,6},{10,8},{12,10},{14,12},{16,14},{18,16},{20... | collective-permute-start | bytes 24584 | tf_op jit(solution)/shard_map/ppermute | solution.py:26
  72.5 7.4 %collective-permute-start.12 = (f32[1,4,32]{1,0,2:T(1,128)S(1)}, f32[1,4,32]{1,0,2:T(1,128)S(1)}, u32[]{:S(2)}, u32[]{:S(2)}) collective-permute-start(f32[1,4,32]{1,0,2:T(1,128)S(1)} %slice.1326), channel_id=1, source_target_pairs={{0,2},{2,4},{4,6},{6,8},{8,10},{10,12},{12,14},{14,16},{16,18},{18... | collective-permute-start | bytes 1544 | tf_op jit(solution)/shard_map/ppermute | solution.py:23
  80.0 3.8 %collective-permute-start.13 = (f32[1,4,32]{1,0,2:T(1,128)S(1)}, f32[1,4,32]{1,0,2:T(1,128)S(1)}, u32[]{:S(2)}, u32[]{:S(2)}) collective-permute-start(f32[1,4,32]{1,0,2:T(1,128)S(1)} %get-tuple-element.374), channel_id=1, source_target_pairs={{2,0},{4,2},{6,4},{8,6},{10,8},{12,10},{14,12},{16,14},{18,16},{20... | collective-permute-start | bytes 1544 | tf_op jit(solution)/shard_map/ppermute | solution.py:26
  84.0 1.3 collective-permute-start.14
  85.3 1.3 collective-permute-start.15
  94.4 13.4 %all-to-all-start = ((f32[16,2,2]{1,2,0:T(2,128)}), f32[16,2,2]{1,2,0:T(2,128)S(1)}, u32[]{:S(2)}, u32[]{:S(2)}) async-start(f32[16,2,2]{1,2,0:T(2,128)} %bitcast.39), calls=%async_computation | async-start | bytes 32768 | tf_op jit(solution)/shard_map/all_to_all | solution.py:165
  107.8 3.6 %collective-permute-start.17 = (f32[1,2,32]{2,1,0:T(2,128)S(1)}, f32[1,2,32]{2,1,0:T(2,128)S(1)}, u32[]{:S(2)}, u32[]{:S(2)}) collective-permute-start(f32[1,2,32]{2,1,0:T(2,128)S(1)} %copy.342), channel_id=1, source_target_pairs={{2,0},{4,2},{6,4},{8,6},{10,8},{12,10},{14,12},{16,14},{18,16},{20... | collective-permute-start | bytes 776 | tf_op jit(solution)/shard_map/ppermute | solution.py:26
  108.5 7.2 %collective-permute-start.16 = (f32[1,2,32]{2,1,0:T(2,128)S(1)}, f32[1,2,32]{2,1,0:T(2,128)S(1)}, u32[]{:S(2)}, u32[]{:S(2)}) collective-permute-start(f32[1,2,32]{2,1,0:T(2,128)S(1)} %copy.342), channel_id=1, source_target_pairs={{0,2},{2,4},{4,6},{6,8},{8,10},{10,12},{12,14},{14,16},{16,18},{18... | collective-permute-start | bytes 776 | tf_op jit(solution)/shard_map/ppermute | solution.py:23
  117.9 10.8 %all-to-all-start.1 = ((f32[1,2,32]{1,0,2:T(1,128)}), f32[1,2,32]{1,0,2:T(1,128)S(1)}, u32[]{:S(2)}, u32[]{:S(2)}) async-start(f32[1,2,32]{1,0,2:T(1,128)} %copy.253), calls=%async_computation.1 | async-start | bytes 32768 | tf_op jit(solution)/shard_map/all_to_all | solution.py:178
  139.0 7.4 %collective-permute-start.18 = (f32[1,4,32]{1,0,2:T(1,128)S(1)}, f32[1,4,32]{1,0,2:T(1,128)S(1)}, u32[]{:S(2)}, u32[]{:S(2)}) collective-permute-start(f32[1,4,32]{1,0,2:T(1,128)S(1)} %slice.1344), channel_id=1, source_target_pairs={{0,2},{2,4},{4,6},{6,8},{8,10},{10,12},{12,14},{14,16},{16,18},{18... | collective-permute-start | bytes 1544 | tf_op jit(solution)/shard_map/ppermute | solution.py:23
  146.4 3.8 %collective-permute-start.19 = (f32[1,4,32]{1,0,2:T(1,128)S(1)}, f32[1,4,32]{1,0,2:T(1,128)S(1)}, u32[]{:S(2)}, u32[]{:S(2)}) collective-permute-start(f32[1,4,32]{1,0,2:T(1,128)S(1)} %get-tuple-element.370), channel_id=1, source_target_pairs={{2,0},{4,2},{6,4},{8,6},{10,8},{12,10},{14,12},{16,14},{18,16},{20... | collective-permute-start | bytes 1544 | tf_op jit(solution)/shard_map/ppermute | solution.py:26
  150.5 1.3 collective-permute-start.20
  151.8 1.3 collective-permute-start.21
  166.4 7.3 %collective-permute-start.22 = (f32[1,16,128]{2,0,1:T(1,128)S(1)}, f32[1,16,128]{2,0,1:T(1,128)S(1)}, u32[]{:S(2)}, u32[]{:S(2)}) collective-permute-start(f32[1,16,128]{2,0,1:T(1,128)S(1)} %slice.1362), channel_id=1, source_target_pairs={{0,2},{2,4},{4,6},{6,8},{8,10},{10,12},{12,14},{14,16},{16,18},{18... | collective-permute-start | bytes 24584 | tf_op jit(solution)/shard_map/ppermute | solution.py:23
  173.7 3.7 %collective-permute-start.23 = (f32[1,16,128]{2,0,1:T(1,128)S(1)}, f32[1,16,128]{2,0,1:T(1,128)S(1)}, u32[]{:S(2)}, u32[]{:S(2)}) collective-permute-start(f32[1,16,128]{2,0,1:T(1,128)S(1)} %get-tuple-element.352), channel_id=1, source_target_pairs={{2,0},{4,2},{6,4},{8,6},{10,8},{12,10},{14,12},{16,14},{18,16},{20... | collective-permute-start | bytes 24584 | tf_op jit(solution)/shard_map/ppermute | solution.py:26
  190.0 7.3 %collective-permute-start.26 = (f32[1,16,128]{2,0,1:T(1,128)S(1)}, f32[1,16,128]{2,0,1:T(1,128)S(1)}, u32[]{:S(2)}, u32[]{:S(2)}) collective-permute-start(f32[1,16,128]{2,0,1:T(1,128)S(1)} %slice.1380), channel_id=1, source_target_pairs={{0,2},{2,4},{4,6},{6,8},{8,10},{10,12},{12,14},{14,16},{16,18},{18... | collective-permute-start | bytes 24584 | tf_op jit(solution)/shard_map/ppermute | solution.py:23
  197.3 3.7 %collective-permute-start.27 = (f32[1,16,128]{2,0,1:T(1,128)S(1)}, f32[1,16,128]{2,0,1:T(1,128)S(1)}, u32[]{:S(2)}, u32[]{:S(2)}) collective-permute-start(f32[1,16,128]{2,0,1:T(1,128)S(1)} %get-tuple-element.348), channel_id=1, source_target_pairs={{2,0},{4,2},{6,4},{8,6},{10,8},{12,10},{14,12},{16,14},{18,16},{20... | collective-permute-start | bytes 24584 | tf_op jit(solution)/shard_map/ppermute | solution.py:26
  (24 other events, 47.5 us)
where the time goes:
time: 205 us; the launch traced here: 204 us
  waiting for transfers between devices  85 us (41%)
  local copies, waits for them, and re-layouts  75.8 us (37%)
  starting transfers between devices  27 us (13%)
  matrix products  9.54 us (5%)
  other arithmetic  4.21 us (2%)
  between operations  2.73 us (1%)
    ppermute x15, waiting for transfers between devices, extended(): lax.ppermute(lax.slice_in_dim(block, block.shape[dim] - width, None, axis...  46 us
    scatter x61, local copies, waits for them, and re-layouts, pair_sum(): return field.at[pick(count - 1)].set(new_last).at[pick(0)].set(new_first)  36.4 us
    ppermute x15, waiting for transfers between devices, extended(): lax.ppermute(lax.slice_in_dim(block, 0, width, axis=dim), axis, backward)  24.8 us
    ppermute x15, starting transfers between devices, extended(): lax.ppermute(lax.slice_in_dim(block, 0, width, axis=dim), axis, backward)  9.93 us
    ppermute x15, starting transfers between devices, extended(): lax.ppermute(lax.slice_in_dim(block, block.shape[dim] - width, None, axis...  7.31 us
    all_to_all x1, waiting for transfers between devices, local(): lax.all_to_all(jnp.transpose(vertices, (2, 1, 0)), 'wide', split_axis=0,...  7.3 us
    all_to_all x1, waiting for transfers between devices, local(): lax.all_to_all(coarse_product, 'wide', split_axis=2, concat_axis=0, tiled...  6.92 us
    all_to_all x1, starting transfers between devices, local(): lax.all_to_all(jnp.transpose(vertices, (2, 1, 0)), 'wide', split_axis=0,...  6.01 us
  transfers between devices with their start and end apart: 32, of which 28 were waited for; matrix products, arithmetic and copies ran while one was open for 7% of the time, Pallas kernels for 0%

commit v1 on v0

v1 whole, which is shorter than its diff:
```python
import functools

import jax
import jax.numpy as jnp
import numpy as np
from jax import lax
from jax.experimental import pallas as pl
from jax.experimental.pallas import tpu as pltpu
from jax.sharding import PartitionSpec as P

NP = 8
K = 8
BS = 8
MESH = pl.DeviceIdType.MESH
F32 = jnp.float32
BF16 = jnp.bfloat16

upper_bound = 6.0
lower_bound = 0.6
centre = (upper_bound + lower_bound) / 2.0
half_width = (upper_bound - lower_bound) / 2.0
aspect = centre / half_width
first_weight = 1.0 / aspect
second_weight = 1.0 / (2.0 * aspect - first_weight)


def gll_tables(count):
    order = count - 1
    nodes = np.cos(np.pi * np.arange(count) / order)
    legendre = np.zeros((count, count))
    for sweep in range(101):
        legendre[:, 0] = 1.0
        legendre[:, 1] = nodes
        for degree in range(2, count):
            legendre[:, degree] = (
                (2 * degree - 1) * nodes * legendre[:, degree - 1]
                - (degree - 1) * legendre[:, degree - 2]
            ) / degree
        if sweep < 100:
            nodes = nodes - (nodes * legendre[:, order] - legendre[:, order - 1]) / (
                count * legendre[:, order]
            )
    nodes = nodes[::-1].copy()
    values = legendre[::-1, order].copy()
    identity_table = np.eye(count)
    spacing = nodes[:, None] - nodes[None, :] + identity_table
    derivative = values[:, None] / values[None, :] / spacing
    derivative = derivative * (1.0 - identity_table)
    derivative[0, 0] = -order * (order + 1) / 4.0
    derivative[-1, -1] = order * (order + 1) / 4.0
    linear = np.stack([(1.0 - nodes) / 2.0, (1.0 + nodes) / 2.0], axis=1)
    return derivative.astype(np.float32), linear.astype(np.float32)


def stacked_pieces(table):
    high = table.astype(jnp.bfloat16)
    low = (table - high.astype(np.float32)).astype(jnp.bfloat16)
    row = np.concatenate([high, low], axis=1)
    return np.concatenate([row, row], axis=0)


def tables_of(nw, nz):
    deriv, lin = gll_tables(NP)
    eye = np.eye(16, dtype=np.float32)
    square = deriv * deriv
    z_tables = np.stack(
        [
            stacked_pieces(np.kron(eye, deriv.T)),
            stacked_pieces(np.kron(eye, deriv)),
            stacked_pieces(np.kron(eye, square)),
        ]
    )
    node = np.arange(8)
    y_table = np.zeros((3, 8, 8, 128), np.float32)
    for shift in range(8):
        other = (node - shift) % 8
        y_table[0, shift] = deriv[node, other][:, None]
        y_table[1, shift] = deriv[other, node][:, None]
        y_table[2, shift] = square[other, node][:, None]
    three = np.zeros((3, 16), np.float32)
    three[0, :8] = lin[:, 0]
    three[1, :8] = lin[:, 1]
    three[1, 8:] = lin[:, 0]
    three[2, 8:] = lin[:, 1]
    corner = np.zeros((128, 256), np.float32)
    for layer in range(3):
        for yv in range(3):
            for xv in range(3):
                corner[layer * 16 + yv * 4 + xv] = np.kron(three[xv], three[yv])
    wz = np.zeros((nw, nz), np.float32)
    for v in range(nw):
        wz[v, v * 8 : v * 8 + 8] += lin[:, 0]
        back = (v - 1) % nw
        wz[v, back * 8 : back * 8 + 8] += lin[:, 1]
    wz3 = np.concatenate([np.roll(wz, 1, axis=0), wz, np.roll(wz, -1, axis=0)], axis=0)
    nb = 2 * (2 * nw // BS)
    rep = np.kron(np.eye(nb, dtype=np.float32), np.ones((1, 8), np.float32))
    pick = np.zeros((2 * nw, 8), np.float32)
    for par in range(2):
        for w in range(nw):
            pick[par * nw + w, 2 * (w % 4) + par] = 1.0
    return deriv, (
        jnp.asarray(z_tables),
        jnp.asarray(y_table),
        jnp.asarray(corner[:64]),
        jnp.asarray(wz3),
        jnp.asarray(rep),
        jnp.asarray(pick),
        jnp.asarray(np.ascontiguousarray(corner[:16].T)),
    )


def halves(value):
    high = value.astype(BF16)
    return high, (value - high.astype(F32)).astype(BF16)


def mm(a, b, transposed=False):
    dims = (((1,), (1 if transposed else 0,)), ((), ()))
    dot = functools.partial(lax.dot_general, dimension_numbers=dims, preferred_element_type=F32)
    ah, al = halves(a)
    bh, bl = halves(b)
    return dot(ah, bh) + (dot(al, bh) + dot(ah, bl))


def kernel(
    nw, nd, deriv,
    rhs_ref, metric_ref, helm_ref, columns_ref, live_ref, values_ref,
    zt_ref, yt_ref, corner_ref, wz3_ref, rep_ref, pick_ref, expand_ref,
    out_ref, product_ref,
    xs, ys, es, xr, yr, er, qs, qr, cs, cr, inv_ref, m_ref, spread_ref,
    face_send, face_recv, q_send, q_recv, c_send, c_recv,
):
    nz = rhs_ref.shape[2]
    nxb = 2 * nw // BS
    nb = 2 * nxb
    width = nb * 8
    w = lax.axis_index("wide")
    d = lax.axis_index("deep")
    left, right = lax.rem(w + nw - 1, nw), lax.rem(w + 1, nw)
    down, up = lax.rem(d + nd - 1, nd), lax.rem(d + 1, nd)
    around = [up] if nd == 2 else [down, up]

    barrier = pltpu.get_barrier_semaphore()

    def greet(step, carry):
        to = lax.rem(w + step, nw)
        for other in around:
            pl.semaphore_signal(
                barrier, inc=1, device_id={"wide": to, "deep": other}, device_id_type=MESH
            )

        @pl.when(step > 0)
        def _():
            pl.semaphore_signal(
                barrier, inc=1, device_id={"wide": to, "deep": d}, device_id_type=MESH
            )

        return carry

    lax.fori_loop(0, nw, greet, 0)

    rows = lax.broadcasted_iota(jnp.int32, (16, 8, nz), 1)
    lanes = lax.broadcasted_iota(jnp.int32, (16, 16, nz), 2) % 8
    plane = lax.broadcasted_iota(jnp.int32, (16, nz), 0)

    def local_sum(f):
        after = pltpu.roll(f.reshape(256, nz), nz - 1, 1).reshape(16, 16, nz)
        before = pltpu.roll(f.reshape(256, nz), 1, 1).reshape(16, 16, nz)
        f = f + jnp.where(lanes == 7, after, jnp.where(lanes == 0, before, 0.0))
        lo, hi = f[:, :8], f[:, 8:]
        new_lo = lo + jnp.where(rows == 7, pltpu.roll(hi, 7, 1), 0.0)
        new_hi = hi + jnp.where(rows == 0, pltpu.roll(lo, 1, 1), 0.0)
        f = jnp.concatenate([new_lo, new_hi], axis=1)
        shared = f[7:8] + f[8:9]
        return jnp.concatenate([f[:7], shared, shared, f[9:]], axis=0)

    def face_copies(turn):
        pairs = [
            (xs.at[turn, 1], xr.at[turn, 0], right, d),
            (xs.at[turn, 0], xr.at[turn, 1], left, d),
            (ys.at[turn, 1], yr.at[turn, 0], w, up),
            (ys.at[turn, 0], yr.at[turn, 1], w, down),
            (es.at[turn, 3], er.at[turn, 0], right, up),
            (es.at[turn, 2], er.at[turn, 1], right, down),
            (es.at[turn, 1], er.at[turn, 2], left, up),
            (es.at[turn, 0], er.at[turn, 3], left, down),
        ]
        return [
            pltpu.make_async_remote_copy(
                src_ref=src,
                dst_ref=dst,
                send_sem=face_send.at[turn, index],
                recv_sem=face_recv.at[turn, index],
                device_id={"wide": to_w, "deep": to_d},
                device_id_type=MESH,
            )
            for index, (src, dst, to_w, to_d) in enumerate(pairs)
        ]

    def begin(turn, f):
        f = local_sum(f)
        xs[turn, 0] = f[0]
        xs[turn, 1] = f[15]
        ys[turn, 0] = f[:, 0:1]
        ys[turn, 1] = f[:, 15:16]
        es[turn, 0] = f[0, 0:1]
        es[turn, 1] = f[0, 15:16]
        es[turn, 2] = f[15, 0:1]
        es[turn, 3] = f[15, 15:16]
        copies = face_copies(turn)
        for copy in copies:
            copy.start()
        return f, copies

    def finish(turn, f, copies):
        for copy in copies:
            copy.wait_recv()
        lo = f[:, :8] + jnp.where(rows == 0, yr[turn, 0], 0.0)
        hi = f[:, 8:] + jnp.where(rows == 7, yr[turn, 1], 0.0)
        f = jnp.concatenate([lo, hi], axis=1)

        def face(side):
            edge_lo, edge_hi = er[turn, 2 * side], er[turn, 2 * side + 1]
            return xr[turn, side] + jnp.where(
                plane == 0, edge_lo, jnp.where(plane == 15, edge_hi, 0.0)
            )

        return jnp.concatenate(
            [f[:1] + face(0)[None], f[1:15], f[15:] + face(1)[None]], axis=0
        )

    def x_apply(u, table):
        parts = u.reshape(2, 8, 16, nz)
        nodes = [parts[:, i] for i in range(8)]
        result = []
        for m in range(8):
            total = float(table[m, 0]) * nodes[0]
            for i in range(1, 8):
                total = total + float(table[m, i]) * nodes[i]
            result.append(total)
        return jnp.stack(result, axis=1).reshape(16, 16, nz)

    def y_apply(u, which):
        parts = u.reshape(32, 8, nz)

        def coefficient(shift):
            table = yt_ref[which, shift]
            if nz > 128:
                table = jnp.concatenate([table] * (nz // 128), axis=1)
            return table[None]

        total = coefficient(0) * parts
        for shift in range(1, 8):
            total = total + coefficient(shift) * pltpu.roll(parts, shift, 1)
        return total.reshape(16, 16, nz)

    def z_apply(u, which):
        flat = u.reshape(256, nz)
        result = []
        for start in range(0, nz, 128):
            high, low = halves(flat[:, start : start + 128])
            both = jnp.dot(
                jnp.concatenate([high, low], axis=1), zt_ref[which], preferred_element_type=F32
            )
            result.append(both[:, :128] + both[:, 128:])
        whole = result[0] if len(result) == 1 else jnp.concatenate(result, axis=1)
        return whole.reshape(16, 16, nz)

    def operator(u):
        total = helm_ref[...] * u
        total = total + x_apply(metric_ref[0] * x_apply(u, deriv), deriv.T)
        total = total + y_apply(metric_ref[1] * y_apply(u, 0), 1)
        return total + z_apply(metric_ref[2] * z_apply(u, 0), 1)

    square = deriv * deriv
    diagonal = helm_ref[...] + x_apply(metric_ref[0], square.T)
    diagonal = diagonal + y_apply(metric_ref[1], 2) + z_apply(metric_ref[2], 2)

    pl.semaphore_wait(barrier, nw * (1 + len(around)) - 1)
    diagonal, diagonal_copies = begin(0, diagonal)
    summed, rhs_copies = begin(1, rhs_ref[...])

    v = jnp.concatenate([values_ref[0, y] for y in range(2)], axis=0)
    spread = mm(v.T, rep_ref[...]).reshape(K, BS, BS, width)
    slot_lane = lax.broadcasted_iota(jnp.int32, (BS, width), 1) % 8
    cols = jnp.concatenate([columns_ref[0, y] for y in range(2)], axis=0).astype(F32)
    live = jnp.concatenate(
        [jnp.concatenate([live_ref[0, y : y + 1, b : b + 1] for b in range(nxb)], axis=0) for y in range(2)],
        axis=0,
    )
    slot = lax.broadcasted_iota(jnp.int32, (nb, K), 1)
    cols = jnp.where(slot < live, cols, -1.0)
    cols = jnp.dot(
        cols.T.astype(BF16), rep_ref[...].astype(BF16), preferred_element_type=F32
    ).astype(jnp.int32)
    block = lax.broadcasted_iota(jnp.int32, (nw, width), 0) // 4
    sums = [jnp.zeros((nw, width), F32) for _ in range(12)]
    for k in range(K):
        chosen = jnp.zeros((BS, width), F32)
        for i in range(BS):
            chosen = chosen + jnp.where(slot_lane == i, spread[k, i], 0.0)
        placed = mm(pick_ref[...], chosen)
        for layer in range(3):
            for y in range(2):
                hit = cols[k : k + 1] == block + (layer * nb + y * nxb)
                for par in range(2):
                    at = layer * 4 + y * 2 + par
                    sums[at] = sums[at] + jnp.where(
                        hit, placed[par * nw : (par + 1) * nw], 0.0
                    )
    for at in range(12):
        m_ref[at] = sums[at]

    vertex = lax.broadcasted_iota(jnp.int32, (16, 2 * width), 0)
    lane = lax.broadcasted_iota(jnp.int32, (16, 2 * width), 1)
    yv, xv = vertex // 4, vertex % 4
    wanted_x = lax.rem(2 * w + xv, 2 * nw)
    wanted = jnp.where(yv < 2, yv * 2 * nw, width) + wanted_x
    selected = jnp.where((lane == wanted) & (yv < 3) & (xv < 3), 1.0, 0.0)
    spread_ref[...] = mm(expand_ref[...], selected)

    inverse = 1.0 / finish(0, diagonal, diagonal_copies)
    inv_ref[...] = inverse
    residual = finish(1, summed, rhs_copies)
    update = inverse * residual * (1.0 / centre)
    u = update
    f, face_two = begin(2, rhs_ref[...] - operator(u))
    residual = finish(2, f, face_two)
    update = (second_weight * first_weight) * update + (
        (2.0 * second_weight / half_width) * inv_ref[...]
    ) * residual
    first = u + update

    local_res = rhs_ref[...] - operator(first)
    vertices = mm(corner_ref[...], local_res.reshape(256, nz))
    shifted = mm(wz3_ref[...], vertices, True)
    group = lax.broadcasted_iota(jnp.int32, (nw, 64), 1) // 16
    packed = jnp.where(
        group == 0,
        shifted[:nw],
        jnp.where(group == 1, shifted[nw : 2 * nw], shifted[2 * nw :]),
    )
    packed = jnp.concatenate([packed, jnp.zeros((nw, 64), F32)], axis=1)
    for row in range(nw):
        qs[row] = packed[row : row + 1]
    qr[0, w] = qs[w]

    def q_copy(to, to_d, which):
        return pltpu.make_async_remote_copy(
            src_ref=qs.at[to],
            dst_ref=qr.at[which, w],
            send_sem=q_send.at[which],
            recv_sem=q_recv.at[which],
            device_id={"wide": to, "deep": to_d},
            device_id_type=MESH,
        )

    def q_start(step, carry):
        to = lax.rem(w + step, nw)
        q_copy(to, up, 1).start()

        @pl.when(step > 0)
        def _():
            q_copy(to, d, 0).start()

        return carry

    lax.fori_loop(0, nw, q_start, 0)

    def wait_rows(ref, count, which, semaphore):
        view = ref.at[which, pl.ds(0, count)]
        pltpu.make_async_copy(view, view, semaphore).wait()

    wait_rows(qr, nw - 1, 0, q_recv.at[0])
    wait_rows(qr, nw, 1, q_recv.at[1])
    own = jnp.concatenate([qr[0, row] for row in range(nw)], axis=0)
    below = jnp.concatenate([qr[1, row] for row in range(nw)], axis=0)
    frame = own + pltpu.roll(below, 128 - 8, 1)
    frame = frame + pltpu.roll(pltpu.roll(frame, 1, 0), 128 - 2, 1)
    total = jnp.zeros((nw, width), F32)
    for layer in range(3):
        for y in range(2):
            for par in range(2):
                at = layer * 16 + y * 4 + par
                total = total + m_ref[layer * 4 + y * 2 + par] * frame[:, at : at + 1]
    product = jnp.sum(total, axis=0, keepdims=True)
    cs[0] = product
    cr[0, w] = product
    product_ref[0, 0:1] = product[:, : 2 * nw]
    product_ref[0, 1:2] = product[:, 2 * nw :]

    def c_copy(to, to_d, which):
        return pltpu.make_async_remote_copy(
            src_ref=cs.at[0],
            dst_ref=cr.at[which, w],
            send_sem=c_send.at[which],
            recv_sem=c_recv.at[which],
            device_id={"wide": to, "deep": to_d},
            device_id_type=MESH,
        )

    def c_start(step, carry):
        to = lax.rem(w + step, nw)
        c_copy(to, down, 1).start()

        @pl.when(step > 0)
        def _():
            c_copy(to, d, 0).start()

        return carry

    lax.fori_loop(0, nw, c_start, 0)
    wait_rows(cr, nw - 1, 0, c_recv.at[0])
    wait_rows(cr, nw, 1, c_recv.at[1])
    mine = jnp.concatenate([cr[0, row] for row in range(nw)], axis=0)
    above = jnp.concatenate([cr[1, row] for row in range(nw)], axis=0)
    both = jnp.concatenate([mine, above], axis=1)
    correction = mm(mm(spread_ref[...], both, True), wz3_ref[nw : 2 * nw])
    u = first + correction.reshape(16, 16, nz)

    f, face_three = begin(3, rhs_ref[...] - operator(u))
    update = inv_ref[...] * finish(3, f, face_three) * (1.0 / centre)
    u = u + update
    f, face_four = begin(4, rhs_ref[...] - operator(u))
    residual = finish(4, f, face_four)
    update = (second_weight * first_weight) * update + (
        (2.0 * second_weight / half_width) * inv_ref[...]
    ) * residual
    out_ref[...] = u + update

    for copies in (diagonal_copies, rhs_copies, face_two, face_three, face_four):
        for copy in copies:
            copy.wait_send()
    wait_rows(qr, nw - 1, 0, q_send.at[0])
    wait_rows(qr, nw, 1, q_send.at[1])
    wait_rows(cr, nw - 1, 0, c_send.at[0])
    wait_rows(cr, nw, 1, c_send.at[1])


def local(nw, nd, *arguments):
    rhs = arguments[0]
    nz = rhs.shape[2]
    deriv, tables = tables_of(nw, nz)
    width = 4 * nw
    vmem = pl.BlockSpec(memory_space=pltpu.VMEM)
    return pl.pallas_call(
        functools.partial(kernel, nw, nd, deriv),
        out_shape=(
            jax.ShapeDtypeStruct(rhs.shape, F32),
            jax.ShapeDtypeStruct((1, 2, 2 * nw), F32),
        ),
        in_specs=[vmem] * 13,
        out_specs=(vmem, vmem),
        scratch_shapes=[
            pltpu.VMEM((5, 2, 16, nz), F32),
            pltpu.VMEM((5, 2, 16, 1, nz), F32),
            pltpu.VMEM((5, 4, 1, nz), F32),
            pltpu.VMEM((5, 2, 16, nz), F32),
            pltpu.VMEM((5, 2, 16, 1, nz), F32),
            pltpu.VMEM((5, 4, 1, nz), F32),
            pltpu.VMEM((nw, 1, 128), F32),
            pltpu.VMEM((2, nw, 1, 128), F32),
            pltpu.VMEM((1, 1, width), F32),
            pltpu.VMEM((2, nw, 1, width), F32),
            pltpu.VMEM((16, 16, nz), F32),
            pltpu.VMEM((12, nw, width), F32),
            pltpu.VMEM((256, 2 * width), F32),
            pltpu.SemaphoreType.DMA((5, 8)),
            pltpu.SemaphoreType.DMA((5, 8)),
            pltpu.SemaphoreType.DMA((2,)),
            pltpu.SemaphoreType.DMA((2,)),
            pltpu.SemaphoreType.DMA((2,)),
            pltpu.SemaphoreType.DMA((2,)),
        ],
        compiler_params=pltpu.CompilerParams(
            collective_id=0, has_side_effects=True, vmem_limit_bytes=48 * 1024 * 1024
        ),
    )(*arguments, *tables)


def solution(mesh):
    placed = (
        P("wide", "deep", None),
        P(None, "wide", "deep", None),
        P("wide", "deep", None),
        P("wide", "deep", None, None),
        P("wide", "deep", None),
        P("wide", "deep", None, None),
    )
    return jax.shard_map(
        functools.partial(local, mesh.shape["wide"], mesh.shape["deep"]),
        mesh=mesh,
        in_specs=placed,
        out_specs=(P("wide", "deep", None), P("wide", "deep", None)),
        check_vma=False,
    )
```

time: 205 us -> 51.5 us (0.25)
  waiting for transfers between devices: 85 us -> 0 us
  local copies, waits for them, and re-layouts: 75.8 us -> 11.9 us
  Pallas kernels: 0 us -> 38.4 us
  starting transfers between devices: 27 us -> 0 us
  matrix products: 9.54 us -> 0 us
  other arithmetic: 4.21 us -> 0 us
  between operations: 2.73 us -> 0.66 us
    ppermute x30 -> x0, waiting for transfers between devices: 70.8 us -> none  [the longest x15 46 us: extended(): lax.ppermute(lax.slice_in_dim(block, block.shape[dim] - width, None, axis...]
    scatter x62 -> x0, local copies, waits for them, and re-layouts: 40.8 us -> none  [the longest x61 36.4 us: pair_sum(): return field.at[pick(count - 1)].set(new_last).at[pick(0)].set(new_first)]
    pallas_call x0 -> x1, Pallas kernels: none -> 38.4 us  [local(): pl.pallas_call(functools.partial(kernel, nw, nd, deriv), out_shape=(jax.S...]
    ppermute x30 -> x0, starting transfers between devices: 17.2 us -> none  [the longest x15 9.93 us: extended(): lax.ppermute(lax.slice_in_dim(block, 0, width, axis=dim), axis, backward)]
    slice x69 -> x0, local copies, waits for them, and re-layouts: 16 us -> none  [the longest x1 5.24 us: local(): vertices = assembled[::2, ::2, ::2]]
    all_to_all x2 -> x0, waiting for transfers between devices: 14.2 us -> none  [the longest x1 7.3 us: local(): lax.all_to_all(jnp.transpose(vertices, (2, 1, 0)), 'wide', split_axis=0,...]
    all_to_all x2 -> x0, starting transfers between devices: 9.73 us -> none  [the longest x1 6.01 us: local(): lax.all_to_all(jnp.transpose(vertices, (2, 1, 0)), 'wide', split_axis=0,...]
    dot_general x34 -> x0, matrix products: 9.54 us -> none  [the longest x11 3.06 us: contract(): return jnp.einsum('mi,iyz->myz', table, field, precision=highest)]
  transfers between devices with their start and end apart: 32 -> 0, of which waited for: 28 -> 0; matrix products, arithmetic and copies ran while one was open for 7% -> 0% of each run, Pallas kernels for 0% -> 0%
where the time goes in v1:
time: 51.5 us; the launch traced here: 50.9 us
  Pallas kernels  38.4 us (75%)
  local copies, waits for them, and re-layouts  11.9 us (23%)
  between operations  0.66 us (1%)
    pallas_call x1, Pallas kernels, local(): pl.pallas_call(functools.partial(kernel, nw, nd, deriv), out_shape=(jax.S...  38.4 us
    unnamed x28, local copies, waits for them, and re-layouts  11.9 us

profile of v1, /device:TPU:0, one launch (start us, length us, event | category | flops | bytes accessed | tf_op | source)
XLA Modules:
  0.0 50.9 jit_solution(2025740807571008401)
XLA Ops:
  0.6 0.0 copy-start.11
  0.6 0.7 %copy-done.11 = f32[8,64]{1,0:T(8,128)S(1)} copy-done((f32[8,64]{1,0:T(8,128)S(1)}, f32[8,64]{1,0:T(8,128)}, u32[]{:S(2)}) %copy-start.11) | copy-done | bytes 2072
  1.3 0.0 copy-start
  1.3 1.0 %copy-done = f32[3,16,16,128]{3,2,1,0:T(8,128)S(1)} copy-done((f32[3,16,16,128]{3,2,1,0:T(8,128)S(1)}, f32[3,16,16,128]{3,2,1,0:T(8,128)}, u32[]{:S(2)}) %copy-start) | copy-done | bytes 393240
  2.3 0.0 copy-start.1
  2.3 1.0 %copy-done.1 = bf16[3,256,256]{2,1,0:T(8,128)(2,1)S(1)} copy-done((bf16[3,256,256]{2,1,0:T(8,128)(2,1)S(1)}, bf16[3,256,256]{2,1,0:T(8,128)(2,1)}, u32[]{:S(2)}) %copy-start.1) | copy-done | bytes 393240
  3.3 0.0 copy-start.2
  3.3 0.9 %copy-done.2 = f32[16,16,128]{2,1,0:T(8,128)S(1)} copy-done((f32[16,16,128]{2,1,0:T(8,128)S(1)}, f32[16,16,128]{2,1,0:T(8,128)}, u32[]{:S(2)}) %copy-start.2) | copy-done | bytes 131096
  4.2 0.0 copy-start.3
  4.2 0.9 %copy-done.3 = f32[16,16,128]{2,1,0:T(8,128)S(1)} copy-done((f32[16,16,128]{2,1,0:T(8,128)S(1)}, f32[16,16,128]{2,1,0:T(8,128)}, u32[]{:S(2)}) %copy-start.3) | copy-done | bytes 131096
  5.1 0.0 copy-start.4
  5.1 0.9 %copy-done.4 = f32[256,16]{1,0:T(8,128)S(1)} copy-done((f32[256,16]{1,0:T(8,128)S(1)}, f32[256,16]{1,0:T(8,128)}, u32[]{:S(2)}) %copy-start.4) | copy-done | bytes 16408
  6.0 0.0 copy-start.5
  6.0 0.9 %copy-done.5 = f32[3,8,8,128]{3,2,1,0:T(8,128)S(1)} copy-done((f32[3,8,8,128]{3,2,1,0:T(8,128)S(1)}, f32[3,8,8,128]{3,2,1,0:T(8,128)}, u32[]{:S(2)}) %copy-start.5) | copy-done | bytes 98328
  6.9 0.0 copy-start.6
  6.9 0.8 %copy-done.6 = f32[64,256]{1,0:T(8,128)S(1)} copy-done((f32[64,256]{1,0:T(8,128)S(1)}, f32[64,256]{1,0:T(8,128)}, u32[]{:S(2)}) %copy-start.6) | copy-done | bytes 65560
  7.8 0.7 %copy-done.7 = f32[48,128]{1,0:T(8,128)S(1)} copy-done((f32[48,128]{1,0:T(8,128)S(1)}, f32[48,128]{1,0:T(8,128)}, u32[]{:S(2)}) %copy-start.7) | copy-done | bytes 24600
  8.5 0.7 %copy-done.8 = f32[1,2,4,512]{3,2,1,0:T(4,128)S(1)} copy-done((f32[1,2,4,512]{3,2,1,0:T(4,128)S(1)}, f32[1,2,4,512]{3,2,1,0:T(4,128)}, u32[]{:S(2)}) %copy-start.8) | copy-done | bytes 16408
  9.2 0.7 %copy-done.9 = f32[32,8]{1,0:T(8,128)S(1)} copy-done((f32[32,8]{1,0:T(8,128)S(1)}, f32[32,8]{1,0:T(8,128)}, u32[]{:S(2)}) %copy-start.9) | copy-done | bytes 1048
  9.9 0.7 %copy-done.10 = s32[1,2,4,8]{3,2,1,0:T(4,128)S(1)} copy-done((s32[1,2,4,8]{3,2,1,0:T(4,128)S(1)}, s32[1,2,4,8]{3,2,1,0:T(4,128)}, u32[]{:S(2)}) %copy-start.10) | copy-done | bytes 280
  10.6 0.7 %copy-done.12 = s32[1,2,4]{2,1,0:T(2,128)S(1)} copy-done((s32[1,2,4]{2,1,0:T(2,128)S(1)}, s32[1,2,4]{2,1,0:T(2,128)}, u32[]{:S(2)}) %copy-start.12) | copy-done | bytes 56
  11.3 38.4 %shard_map.140 = (f32[16,16,128]{2,1,0:T(8,128)S(1)}, f32[1,2,32]{2,1,0:T(2,128)S(1)}) custom-call(f32[16,16,128]{2,1,0:T(8,128)S(1)} %copy-done.2, f32[3,16,16,128]{3,2,1,0:T(8,128)S(1)} %copy-done, f32[16,16,128]{2,1,0:T(8,128)S(1)} %copy-done.3, s32[1,2,4,8]{3,2,1,0:T(4,128)S(1)} %copy-done.10, s32[1,2,4]{2,1,0:T(2,128)S(1)} %copy-done.12, ...), custom_call_target="tpu_custom_call" | custom-call | tf_op jit(solution)/shard_map/pallas_call | solution.py:447
  49.7 0.7 %copy.17 = f32[16,16,128]{2,1,0:T(8,128)} copy(f32[16,16,128]{2,1,0:T(8,128)S(1)} %get-tuple-element.4) | data formatting | bytes 262144
  50.4 0.6 %copy.18 = f32[1,2,32]{2,1,0:T(2,128)} copy(f32[1,2,32]{2,1,0:T(2,128)S(1)} %get-tuple-element.5) | data formatting | bytes 512
  (5 shorter events, 0.0 us)
Async XLA Ops:
  0.6 0.7 %copy-start.11 = (f32[8,64]{1,0:T(8,128)S(1)}, f32[8,64]{1,0:T(8,128)}, u32[]{:S(2)}) copy-start(f32[8,64]{1,0:T(8,128)} %constant.18.clone.rep_ref) | copy-start | bytes 6148
  1.3 1.0 %copy-start = (f32[3,16,16,128]{3,2,1,0:T(8,128)S(1)}, f32[3,16,16,128]{3,2,1,0:T(8,128)}, u32[]{:S(2)}) copy-start(f32[3,16,16,128]{3,2,1,0:T(8,128)} %metric_ref.1) | copy-start | bytes 1179652
  2.3 1.0 %copy-start.1 = (bf16[3,256,256]{2,1,0:T(8,128)(2,1)S(1)}, bf16[3,256,256]{2,1,0:T(8,128)(2,1)}, u32[]{:S(2)}) copy-start(bf16[3,256,256]{2,1,0:T(8,128)(2,1)} %constant.14.clone.zt_ref) | copy-start | bytes 1179652
  3.3 0.9 %copy-start.2 = (f32[16,16,128]{2,1,0:T(8,128)S(1)}, f32[16,16,128]{2,1,0:T(8,128)}, u32[]{:S(2)}) copy-start(f32[16,16,128]{2,1,0:T(8,128)} %rhs_ref.1) | copy-start | bytes 393220
  4.2 0.9 %copy-start.3 = (f32[16,16,128]{2,1,0:T(8,128)S(1)}, f32[16,16,128]{2,1,0:T(8,128)}, u32[]{:S(2)}) copy-start(f32[16,16,128]{2,1,0:T(8,128)} %helm_ref.1) | copy-start | bytes 393220
  5.1 0.9 %copy-start.4 = (f32[256,16]{1,0:T(8,128)S(1)}, f32[256,16]{1,0:T(8,128)}, u32[]{:S(2)}) copy-start(f32[256,16]{1,0:T(8,128)} %constant.20.clone.expand_ref) | copy-start | bytes 49156
  6.0 0.9 %copy-start.5 = (f32[3,8,8,128]{3,2,1,0:T(8,128)S(1)}, f32[3,8,8,128]{3,2,1,0:T(8,128)}, u32[]{:S(2)}) copy-start(f32[3,8,8,128]{3,2,1,0:T(8,128)} %constant.15.clone.yt_ref) | copy-start | bytes 294916
  6.9 0.8 %copy-start.6 = (f32[64,256]{1,0:T(8,128)S(1)}, f32[64,256]{1,0:T(8,128)}, u32[]{:S(2)}) copy-start(f32[64,256]{1,0:T(8,128)} %constant.16.clone.corner_ref) | copy-start | bytes 196612
  7.8 0.7 %copy-start.7 = (f32[48,128]{1,0:T(8,128)S(1)}, f32[48,128]{1,0:T(8,128)}, u32[]{:S(2)}) copy-start(f32[48,128]{1,0:T(8,128)} %constant.17.clone.wz3_ref) | copy-start | bytes 73732
  8.5 0.7 %copy-start.8 = (f32[1,2,4,512]{3,2,1,0:T(4,128)S(1)}, f32[1,2,4,512]{3,2,1,0:T(4,128)}, u32[]{:S(2)}) copy-start(f32[1,2,4,512]{3,2,1,0:T(4,128)} %values_ref.1) | copy-start | bytes 49156
  9.2 0.7 %copy-start.9 = (f32[32,8]{1,0:T(8,128)S(1)}, f32[32,8]{1,0:T(8,128)}, u32[]{:S(2)}) copy-start(f32[32,8]{1,0:T(8,128)} %constant.19.clone.pick_ref) | copy-start | bytes 3076
  9.9 0.7 %copy-start.10 = (s32[1,2,4,8]{3,2,1,0:T(4,128)S(1)}, s32[1,2,4,8]{3,2,1,0:T(4,128)}, u32[]{:S(2)}) copy-start(s32[1,2,4,8]{3,2,1,0:T(4,128)} %columns_ref.1) | copy-start | bytes 772
  10.6 0.7 %copy-start.12 = (s32[1,2,4]{2,1,0:T(2,128)S(1)}, s32[1,2,4]{2,1,0:T(2,128)}, u32[]{:S(2)}) copy-start(s32[1,2,4]{2,1,0:T(2,128)} %live_ref.1) | copy-start | bytes 100

commit v2 on v1

--- a/solution.py
+++ b/solution.py
@@ -125,12 +125,23 @@
 
 def kernel(
     nw, nd, deriv,
-    rhs_ref, metric_ref, helm_ref, columns_ref, live_ref, values_ref,
-    zt_ref, yt_ref, corner_ref, wz3_ref, rep_ref, pick_ref, expand_ref,
-    out_ref, product_ref,
+    *refs,
+):
+    sources, (out_ref, product_ref), held = refs[:13], refs[13:15], refs[15:28]
+    (
+        rhs_ref, metric_ref, helm_ref, columns_ref, live_ref, values_ref,
+        zt_ref, yt_ref, corner_ref, wz3_ref, rep_ref, pick_ref, expand_ref,
+    ) = held
+    (
     xs, ys, es, xr, yr, er, qs, qr, cs, cr, inv_ref, m_ref, spread_ref,
-    face_send, face_recv, q_send, q_recv, c_send, c_recv,
-):
+    face_send, face_recv, q_send, q_recv, c_send, c_recv, load_sem,
+    ) = refs[28:]
+    loads = [
+        pltpu.make_async_copy(source, target, load_sem.at[index])
+        for index, (source, target) in enumerate(zip(sources, held))
+    ]
+    for index in (1, 0, 2, 6, 7, 5, 3, 4, 8, 9, 10, 11, 12):
+        loads[index].start()
     nz = rhs_ref.shape[2]
     nxb = 2 * nw // BS
     nb = 2 * nxb
@@ -273,6 +284,8 @@
         total = total + y_apply(metric_ref[1] * y_apply(u, 0), 1)
         return total + z_apply(metric_ref[2] * z_apply(u, 0), 1)
 
+    for index in (1, 0, 2, 6, 7):
+        loads[index].wait()
     square = deriv * deriv
     diagonal = helm_ref[...] + x_apply(metric_ref[0], square.T)
     diagonal = diagonal + y_apply(metric_ref[1], 2) + z_apply(metric_ref[2], 2)
@@ -280,6 +293,9 @@
     pl.semaphore_wait(barrier, nw * (1 + len(around)) - 1)
     diagonal, diagonal_copies = begin(0, diagonal)
     summed, rhs_copies = begin(1, rhs_ref[...])
+
+    for index in (5, 3, 4, 8, 9, 10, 11, 12):
+        loads[index].wait()
 
     v = jnp.concatenate([values_ref[0, y] for y in range(2)], axis=0)
     spread = mm(v.T, rep_ref[...]).reshape(K, BS, BS, width)
@@ -450,9 +466,10 @@
             jax.ShapeDtypeStruct(rhs.shape, F32),
             jax.ShapeDtypeStruct((1, 2, 2 * nw), F32),
         ),
-        in_specs=[vmem] * 13,
+        in_specs=[pl.BlockSpec(memory_space=pltpu.HBM)] * 13,
         out_specs=(vmem, vmem),
-        scratch_shapes=[
+        scratch_shapes=[pltpu.VMEM(a.shape, a.dtype) for a in (*arguments, *tables)]
+        + [
             pltpu.VMEM((5, 2, 16, nz), F32),
             pltpu.VMEM((5, 2, 16, 1, nz), F32),
             pltpu.VMEM((5, 4, 1, nz), F32),
@@ -472,9 +489,10 @@
             pltpu.SemaphoreType.DMA((2,)),
             pltpu.SemaphoreType.DMA((2,)),
             pltpu.SemaphoreType.DMA((2,)),
+            pltpu.SemaphoreType.DMA((13,)),
         ],
         compiler_params=pltpu.CompilerParams(
-            collective_id=0, has_side_effects=True, vmem_limit_bytes=48 * 1024 * 1024
+            collective_id=0, has_side_effects=True, vmem_limit_bytes=63 * 1024 * 1024
         ),
     )(*arguments, *tables)
 

time: 51.5 us -> 42.1 us (0.82)
  local copies, waits for them, and re-layouts: 11.9 us -> 2.13 us
  Pallas kernels: 38.4 us -> 39.2 us
    unnamed x28 -> x4, local copies, waits for them, and re-layouts: 11.9 us -> 2.13 us
    pallas_call x1, Pallas kernels: 38.4 us -> 39.2 us  [local(): pl.pallas_call(functools.partial(kernel, nw, nd, deriv), out_shape=(jax.S...]
where the time goes in v2:
time: 42.1 us; the launch traced here: 42 us
  Pallas kernels  39.2 us (93%)
  local copies, waits for them, and re-layouts  2.13 us (5%)
  between operations  0.65 us (2%)
    pallas_call x1, Pallas kernels, local(): pl.pallas_call(functools.partial(kernel, nw, nd, deriv), out_shape=(jax.S...  39.2 us
    unnamed x4, local copies, waits for them, and re-layouts  2.13 us

profile of v2, /device:TPU:0, one launch (start us, length us, event | category | flops | bytes accessed | tf_op | source)
XLA Modules:
  0.0 42.0 jit_solution(4847520038763083830)
XLA Ops:
  0.6 39.2 %shard_map.140 = (f32[16,16,128]{2,1,0:T(8,128)}, f32[1,2,32]{2,1,0:T(2,128)}) custom-call(f32[16,16,128]{2,1,0:T(8,128)} %refs_0_.1, f32[3,16,16,128]{3,2,1,0:T(8,128)} %refs_1_.1, f32[16,16,128]{2,1,0:T(8,128)} %refs_2_.1, s32[1,2,4,8]{3,2,1,0:T(4,128)} %refs_3_.1, s32[1,2,4]{2,1,0:T(2,128)} %refs_4_.1, f32[1,2,4,512]{3,2,1,0:T(4,128)} %refs_5_.1, ...), custom_call_target="tpu_custom_call" | custom-call | tf_op jit(solution)/shard_map/pallas_call | solution.py:463
  39.8 0.0 copy-start
  39.8 1.6 %copy.17 = f32[16,16,128]{2,1,0:T(8,128)} copy(f32[16,16,128]{2,1,0:T(8,128)} %get-tuple-element.4) | data formatting | bytes 262144
  41.4 0.0 copy-done
  41.4 0.6 %copy.18 = f32[1,2,32]{2,1,0:T(2,128)} copy(f32[1,2,32]{2,1,0:T(2,128)S(1)} %copy-done) | data formatting | bytes 512
Async XLA Ops:
  39.8 1.6 %copy-start = (f32[1,2,32]{2,1,0:T(2,128)S(1)}, f32[1,2,32]{2,1,0:T(2,128)}, u32[]{:S(2)}) copy-start(f32[1,2,32]{2,1,0:T(2,128)} %get-tuple-element.5) | copy-start | bytes 772

commit v3 on v2

--- a/solution.py
+++ b/solution.py
@@ -87,6 +87,14 @@
         for yv in range(3):
             for xv in range(3):
                 corner[layer * 16 + yv * 4 + xv] = np.kron(three[xv], three[yv])
+    five = np.zeros((5, 32), np.float32)
+    for element in range(4):
+        five[element, element * 8 : element * 8 + 8] = lin[:, 0]
+        five[element + 1, element * 8 : element * 8 + 8] = lin[:, 1]
+    expand = np.zeros((512, 32), np.float32)
+    for yv in range(3):
+        for xv in range(5):
+            expand[:, yv * 8 + xv] = np.kron(five[xv], three[yv])
     wz = np.zeros((nw, nz), np.float32)
     for v in range(nw):
         wz[v, v * 8 : v * 8 + 8] += lin[:, 0]
@@ -106,7 +114,7 @@
         jnp.asarray(wz3),
         jnp.asarray(rep),
         jnp.asarray(pick),
-        jnp.asarray(np.ascontiguousarray(corner[:16].T)),
+        jnp.asarray(expand),
     )
 
 
@@ -133,8 +141,8 @@
         zt_ref, yt_ref, corner_ref, wz3_ref, rep_ref, pick_ref, expand_ref,
     ) = held
     (
-    xs, ys, es, xr, yr, er, qs, qr, cs, cr, inv_ref, m_ref, spread_ref,
-    face_send, face_recv, q_send, q_recv, c_send, c_recv, load_sem,
+    xs, ys, es, xr, yr, er, qs, qr, cs, cr, gm, ls, lr, inv_ref, m_ref, spread_ref,
+    face_send, face_recv, q_send, q_recv, c_send, c_recv, ghost_send, ghost_recv, load_sem,
     ) = refs[28:]
     loads = [
         pltpu.make_async_copy(source, target, load_sem.at[index])
@@ -171,18 +179,23 @@
 
     lax.fori_loop(0, nw, greet, 0)
 
-    rows = lax.broadcasted_iota(jnp.int32, (16, 8, nz), 1)
-    lanes = lax.broadcasted_iota(jnp.int32, (16, 16, nz), 2) % 8
+    row = lax.broadcasted_iota(jnp.int32, (1, 8, nz), 1)
+    lanes = lax.broadcasted_iota(jnp.int32, (1, 16, nz), 2) % 8
     plane = lax.broadcasted_iota(jnp.int32, (16, nz), 0)
 
-    def local_sum(f):
-        after = pltpu.roll(f.reshape(256, nz), nz - 1, 1).reshape(16, 16, nz)
-        before = pltpu.roll(f.reshape(256, nz), 1, 1).reshape(16, 16, nz)
+    def plane_sum(f):
+        count = f.shape[0]
+        flat = f.reshape(count * 16, nz)
+        after = pltpu.roll(flat, nz - 1, 1).reshape(count, 16, nz)
+        before = pltpu.roll(flat, 1, 1).reshape(count, 16, nz)
         f = f + jnp.where(lanes == 7, after, jnp.where(lanes == 0, before, 0.0))
         lo, hi = f[:, :8], f[:, 8:]
-        new_lo = lo + jnp.where(rows == 7, pltpu.roll(hi, 7, 1), 0.0)
-        new_hi = hi + jnp.where(rows == 0, pltpu.roll(lo, 1, 1), 0.0)
-        f = jnp.concatenate([new_lo, new_hi], axis=1)
+        new_lo = lo + jnp.where(row == 7, pltpu.roll(hi, 7, 1), 0.0)
+        new_hi = hi + jnp.where(row == 0, pltpu.roll(lo, 1, 1), 0.0)
+        return jnp.concatenate([new_lo, new_hi], axis=1)
+
+    def local_sum(f):
+        f = plane_sum(f)
         shared = f[7:8] + f[8:9]
         return jnp.concatenate([f[:7], shared, shared, f[9:]], axis=0)
 
@@ -190,8 +203,8 @@
         pairs = [
             (xs.at[turn, 1], xr.at[turn, 0], right, d),
             (xs.at[turn, 0], xr.at[turn, 1], left, d),
-            (ys.at[turn, 1], yr.at[turn, 0], w, up),
-            (ys.at[turn, 0], yr.at[turn, 1], w, down),
+            (ys.at[turn, 1, pl.ds(0, 16)], yr.at[turn, 0, pl.ds(0, 16)], w, up),
+            (ys.at[turn, 0, pl.ds(0, 16)], yr.at[turn, 1, pl.ds(0, 16)], w, down),
             (es.at[turn, 3], er.at[turn, 0], right, up),
             (es.at[turn, 2], er.at[turn, 1], right, down),
             (es.at[turn, 1], er.at[turn, 2], left, up),
@@ -213,8 +226,8 @@
         f = local_sum(f)
         xs[turn, 0] = f[0]
         xs[turn, 1] = f[15]
-        ys[turn, 0] = f[:, 0:1]
-        ys[turn, 1] = f[:, 15:16]
+        ys[turn, 0, 0:16] = f[:, 0:1]
+        ys[turn, 1, 0:16] = f[:, 15:16]
         es[turn, 0] = f[0, 0:1]
         es[turn, 1] = f[0, 15:16]
         es[turn, 2] = f[15, 0:1]
@@ -224,12 +237,38 @@
             copy.start()
         return f, copies
 
+    def add_rows(f, low, high):
+        lo = f[:, :8] + jnp.where(row == 0, low, 0.0)
+        hi = f[:, 8:] + jnp.where(row == 7, high, 0.0)
+        return jnp.concatenate([lo, hi], axis=1)
+
+    def ghost_copy(index, src, dst, to):
+        return pltpu.make_async_remote_copy(
+            src_ref=src,
+            dst_ref=dst,
+            send_sem=ghost_send.at[index],
+            recv_sem=ghost_recv.at[index],
+            device_id={"wide": to, "deep": d},
+            device_id_type=MESH,
+        )
+
+    def ghost_copies():
+        result = []
+        for side, (to, start, face) in enumerate(((right, 8, 15), (left, 0, 0))):
+            pieces = (
+                (metric_ref.at[0, pl.ds(start, 8)], gm.at[side, pl.ds(0, 8)]),
+                (metric_ref.at[1, face], gm.at[side, 8]),
+                (metric_ref.at[2, face], gm.at[side, 9]),
+                (helm_ref.at[face], gm.at[side, 10]),
+            )
+            for index, (src, dst) in enumerate(pieces):
+                result.append(ghost_copy(side * 5 + index, src, dst, to))
+        return result
+
     def finish(turn, f, copies):
         for copy in copies:
             copy.wait_recv()
-        lo = f[:, :8] + jnp.where(rows == 0, yr[turn, 0], 0.0)
-        hi = f[:, 8:] + jnp.where(rows == 7, yr[turn, 1], 0.0)
-        f = jnp.concatenate([lo, hi], axis=1)
+        f = add_rows(f, yr[turn, 0, 0:16], yr[turn, 1, 0:16])
 
         def face(side):
             edge_lo, edge_hi = er[turn, 2 * side], er[turn, 2 * side + 1]
@@ -253,7 +292,7 @@
         return jnp.stack(result, axis=1).reshape(16, 16, nz)
 
     def y_apply(u, which):
-        parts = u.reshape(32, 8, nz)
+        parts = u.reshape(-1, 8, nz)
 
         def coefficient(shift):
             table = yt_ref[which, shift]
@@ -264,10 +303,10 @@
         total = coefficient(0) * parts
         for shift in range(1, 8):
             total = total + coefficient(shift) * pltpu.roll(parts, shift, 1)
-        return total.reshape(16, 16, nz)
+        return total.reshape(u.shape)
 
     def z_apply(u, which):
-        flat = u.reshape(256, nz)
+        flat = u.reshape(-1, nz)
         result = []
         for start in range(0, nz, 128):
             high, low = halves(flat[:, start : start + 128])
@@ -276,7 +315,7 @@
             )
             result.append(both[:, :128] + both[:, 128:])
         whole = result[0] if len(result) == 1 else jnp.concatenate(result, axis=1)
-        return whole.reshape(16, 16, nz)
+        return whole.reshape(u.shape)
 
     def operator(u):
         total = helm_ref[...] * u
@@ -286,6 +325,18 @@
 
     for index in (1, 0, 2, 6, 7):
         loads[index].wait()
+    def ghost_face(side, u, face):
+        nodes = [u[i] for i in range(8)]
+        total = gm[side, 10] * nodes[face]
+        for m in range(8):
+            slope = float(deriv[m, 0]) * nodes[0]
+            for i in range(1, 8):
+                slope = slope + float(deriv[m, i]) * nodes[i]
+            total = total + float(deriv[m, face]) * (gm[side, m] * slope)
+        total = total + y_apply(gm[side, 8] * y_apply(nodes[face], 0), 1)
+        total = total + z_apply(gm[side, 9] * z_apply(nodes[face], 0), 1)
+        return lr[side] - total
+
     square = deriv * deriv
     diagonal = helm_ref[...] + x_apply(metric_ref[0], square.T)
     diagonal = diagonal + y_apply(metric_ref[1], 2) + z_apply(metric_ref[2], 2)
@@ -328,12 +379,12 @@
     for at in range(12):
         m_ref[at] = sums[at]
 
-    vertex = lax.broadcasted_iota(jnp.int32, (16, 2 * width), 0)
-    lane = lax.broadcasted_iota(jnp.int32, (16, 2 * width), 1)
-    yv, xv = vertex // 4, vertex % 4
-    wanted_x = lax.rem(2 * w + xv, 2 * nw)
+    vertex = lax.broadcasted_iota(jnp.int32, (32, 2 * width), 0)
+    lane = lax.broadcasted_iota(jnp.int32, (32, 2 * width), 1)
+    yv, xv = vertex // 8, vertex % 8
+    wanted_x = lax.rem(2 * w - 1 + xv + 2 * nw, 2 * nw)
     wanted = jnp.where(yv < 2, yv * 2 * nw, width) + wanted_x
-    selected = jnp.where((lane == wanted) & (yv < 3) & (xv < 3), 1.0, 0.0)
+    selected = jnp.where((lane == wanted) & (yv < 3) & (xv < 5), 1.0, 0.0)
     spread_ref[...] = mm(expand_ref[...], selected)
 
     inverse = 1.0 / finish(0, diagonal, diagonal_copies)
@@ -342,6 +393,9 @@
     update = inverse * residual * (1.0 / centre)
     u = update
     f, face_two = begin(2, rhs_ref[...] - operator(u))
+    ghosts = ghost_copies()
+    for ghost in ghosts:
+        ghost.start()
     residual = finish(2, f, face_two)
     update = (second_weight * first_weight) * update + (
         (2.0 * second_weight / half_width) * inv_ref[...]
@@ -358,8 +412,8 @@
         jnp.where(group == 1, shifted[nw : 2 * nw], shifted[2 * nw :]),
     )
     packed = jnp.concatenate([packed, jnp.zeros((nw, 64), F32)], axis=1)
-    for row in range(nw):
-        qs[row] = packed[row : row + 1]
+    for at in range(nw):
+        qs[at] = packed[at : at + 1]
     qr[0, w] = qs[w]
 
     def q_copy(to, to_d, which):
@@ -383,6 +437,12 @@
         return carry
 
     lax.fori_loop(0, nw, q_start, 0)
+    ls[0] = local_res[0]
+    ls[1] = local_res[15]
+    faces = [ghost_copy(4, ls.at[1], lr.at[0], right), ghost_copy(9, ls.at[0], lr.at[1], left)]
+    for ghost in faces:
+        ghost.start()
+    ghosts = ghosts + faces
 
     def wait_rows(ref, count, which, semaphore):
         view = ref.at[which, pl.ds(0, count)]
@@ -390,8 +450,8 @@
 
     wait_rows(qr, nw - 1, 0, q_recv.at[0])
     wait_rows(qr, nw, 1, q_recv.at[1])
-    own = jnp.concatenate([qr[0, row] for row in range(nw)], axis=0)
-    below = jnp.concatenate([qr[1, row] for row in range(nw)], axis=0)
+    own = jnp.concatenate([qr[0, at] for at in range(nw)], axis=0)
+    below = jnp.concatenate([qr[1, at] for at in range(nw)], axis=0)
     frame = own + pltpu.roll(below, 128 - 8, 1)
     frame = frame + pltpu.roll(pltpu.roll(frame, 1, 0), 128 - 2, 1)
     total = jnp.zeros((nw, width), F32)
@@ -429,14 +489,42 @@
     lax.fori_loop(0, nw, c_start, 0)
     wait_rows(cr, nw - 1, 0, c_recv.at[0])
     wait_rows(cr, nw, 1, c_recv.at[1])
-    mine = jnp.concatenate([cr[0, row] for row in range(nw)], axis=0)
-    above = jnp.concatenate([cr[1, row] for row in range(nw)], axis=0)
+    mine = jnp.concatenate([cr[0, at] for at in range(nw)], axis=0)
+    above = jnp.concatenate([cr[1, at] for at in range(nw)], axis=0)
     both = jnp.concatenate([mine, above], axis=1)
     correction = mm(mm(spread_ref[...], both, True), wz3_ref[nw : 2 * nw])
-    u = first + correction.reshape(16, 16, nz)
-
-    f, face_three = begin(3, rhs_ref[...] - operator(u))
-    update = inv_ref[...] * finish(3, f, face_three) * (1.0 / centre)
+    for ghost in ghosts:
+        ghost.wait_recv()
+    correction = correction.reshape(32, 16, nz)
+    outer = jnp.stack(
+        [ghost_face(0, correction[:8], 7), ghost_face(1, correction[24:], 0)], axis=0
+    )
+    outer = plane_sum(outer)
+    correction = correction[8:24]
+    u = first + correction
+    f = local_sum(local_res - operator(correction))
+    for side, edge in ((0, 0), (1, 15)):
+        ys[3, side, 0:16] = f[:, edge : edge + 1]
+        ys[3, side, 16:18] = outer[:, edge : edge + 1]
+    face_three = [
+        pltpu.make_async_remote_copy(
+            src_ref=ys.at[3, 1 - side],
+            dst_ref=yr.at[3, side],
+            send_sem=face_send.at[3, side],
+            recv_sem=face_recv.at[3, side],
+            device_id={"wide": w, "deep": to},
+            device_id_type=MESH,
+        )
+        for side, to in ((0, up), (1, down))
+    ]
+    for copy in face_three:
+        copy.start()
+    for copy in face_three:
+        copy.wait_recv()
+    outer = add_rows(outer, yr[3, 0, 16:18], yr[3, 1, 16:18])
+    f = add_rows(f, yr[3, 0, 0:16], yr[3, 1, 0:16])
+    f = jnp.concatenate([f[:1] + outer[:1], f[1:15], f[15:] + outer[1:]], axis=0)
+    update = inv_ref[...] * f * (1.0 / centre)
     u = u + update
     f, face_four = begin(4, rhs_ref[...] - operator(u))
     residual = finish(4, f, face_four)
@@ -445,7 +533,7 @@
     ) * residual
     out_ref[...] = u + update
 
-    for copies in (diagonal_copies, rhs_copies, face_two, face_three, face_four):
+    for copies in (diagonal_copies, rhs_copies, face_two, ghosts, face_three, face_four):
         for copy in copies:
             copy.wait_send()
     wait_rows(qr, nw - 1, 0, q_send.at[0])
@@ -471,24 +559,29 @@
         scratch_shapes=[pltpu.VMEM(a.shape, a.dtype) for a in (*arguments, *tables)]
         + [
             pltpu.VMEM((5, 2, 16, nz), F32),
-            pltpu.VMEM((5, 2, 16, 1, nz), F32),
+            pltpu.VMEM((5, 2, 18, 1, nz), F32),
             pltpu.VMEM((5, 4, 1, nz), F32),
             pltpu.VMEM((5, 2, 16, nz), F32),
-            pltpu.VMEM((5, 2, 16, 1, nz), F32),
+            pltpu.VMEM((5, 2, 18, 1, nz), F32),
             pltpu.VMEM((5, 4, 1, nz), F32),
             pltpu.VMEM((nw, 1, 128), F32),
             pltpu.VMEM((2, nw, 1, 128), F32),
             pltpu.VMEM((1, 1, width), F32),
             pltpu.VMEM((2, nw, 1, width), F32),
+            pltpu.VMEM((2, 11, 16, nz), F32),
+            pltpu.VMEM((2, 16, nz), F32),
+            pltpu.VMEM((2, 16, nz), F32),
             pltpu.VMEM((16, 16, nz), F32),
             pltpu.VMEM((12, nw, width), F32),
-            pltpu.VMEM((256, 2 * width), F32),
+            pltpu.VMEM((512, 2 * width), F32),
             pltpu.SemaphoreType.DMA((5, 8)),
             pltpu.SemaphoreType.DMA((5, 8)),
             pltpu.SemaphoreType.DMA((2,)),
             pltpu.SemaphoreType.DMA((2,)),
             pltpu.SemaphoreType.DMA((2,)),
             pltpu.SemaphoreType.DMA((2,)),
+            pltpu.SemaphoreType.DMA((10,)),
+            pltpu.SemaphoreType.DMA((10,)),
             pltpu.SemaphoreType.DMA((13,)),
         ],
         compiler_params=pltpu.CompilerParams(

time: 42.1 us -> 37.5 us (0.89)
  Pallas kernels: 39.2 us -> 34.6 us
    pallas_call x1, Pallas kernels: 39.2 us -> 34.6 us  [local(): pl.pallas_call(functools.partial(kernel, nw, nd, deriv), out_shape=(jax.S...]
where the time goes in v3:
time: 37.5 us; the launch traced here: 37.4 us
  Pallas kernels  34.6 us (92%)
  local copies, waits for them, and re-layouts  2.13 us (6%)
  between operations  0.65 us (2%)
    pallas_call x1, Pallas kernels, local(): pl.pallas_call(functools.partial(kernel, nw, nd, deriv), out_shape=(jax.S...  34.6 us
    unnamed x4, local copies, waits for them, and re-layouts  2.13 us

profile of v3, /device:TPU:0, one launch (start us, length us, event | category | flops | bytes accessed | tf_op | source)
XLA Modules:
  0.0 37.4 jit_solution(15176428917658524593)
XLA Ops:
  0.6 34.6 %shard_map.140 = (f32[16,16,128]{2,1,0:T(8,128)}, f32[1,2,32]{2,1,0:T(2,128)}) custom-call(f32[16,16,128]{2,1,0:T(8,128)} %refs_0_.1, f32[3,16,16,128]{3,2,1,0:T(8,128)} %refs_1_.1, f32[16,16,128]{2,1,0:T(8,128)} %refs_2_.1, s32[1,2,4,8]{3,2,1,0:T(4,128)} %refs_3_.1, s32[1,2,4]{2,1,0:T(2,128)} %refs_4_.1, f32[1,2,4,512]{3,2,1,0:T(4,128)} %refs_5_.1, ...), custom_call_target="tpu_custom_call" | custom-call | tf_op jit(solution)/shard_map/pallas_call | solution.py:551
  35.2 0.0 copy-start
  35.3 1.6 %copy.17 = f32[16,16,128]{2,1,0:T(8,128)} copy(f32[16,16,128]{2,1,0:T(8,128)} %get-tuple-element.4) | data formatting | bytes 262144
  36.8 0.0 copy-done
  36.8 0.6 %copy.18 = f32[1,2,32]{2,1,0:T(2,128)} copy(f32[1,2,32]{2,1,0:T(2,128)S(1)} %copy-done) | data formatting | bytes 512
Async XLA Ops:
  35.2 1.6 %copy-start = (f32[1,2,32]{2,1,0:T(2,128)S(1)}, f32[1,2,32]{2,1,0:T(2,128)}, u32[]{:S(2)}) copy-start(f32[1,2,32]{2,1,0:T(2,128)} %get-tuple-element.5) | copy-start | bytes 772

commit v4 on v3

--- a/solution.py
+++ b/solution.py
@@ -325,6 +325,35 @@
 
     for index in (1, 0, 2, 6, 7):
         loads[index].wait()
+    def begin_outside_in(turn, u):
+        back = x_apply(metric_ref[0] * x_apply(u, deriv), deriv.T)
+
+        def part(pick):
+            here = pick(u)
+            total = pick(helm_ref[...]) * here + pick(back)
+            total = total + y_apply(pick(metric_ref[1]) * y_apply(here, 0), 1)
+            total = total + z_apply(pick(metric_ref[2]) * z_apply(here, 0), 1)
+            return plane_sum(pick(rhs_ref[...]) - total)
+
+        copies = face_copies(turn)
+        outer = part(lambda v: jnp.concatenate([v[:1], v[15:]], axis=0))
+        for side in range(2):
+            xs[turn, side] = outer[side]
+            es[turn, 2 * side] = outer[side, 0:1]
+            es[turn, 2 * side + 1] = outer[side, 15:16]
+        for index in (0, 1, 4, 5, 6, 7):
+            copies[index].start()
+        inner = part(lambda v: v[1:15])
+        shared = inner[6:7] + inner[7:8]
+        f = jnp.concatenate(
+            [outer[:1], inner[:6], shared, shared, inner[8:], outer[1:]], axis=0
+        )
+        ys[turn, 0, 0:16] = f[:, 0:1]
+        ys[turn, 1, 0:16] = f[:, 15:16]
+        for index in (2, 3):
+            copies[index].start()
+        return f, copies
+
     def ghost_face(side, u, face):
         nodes = [u[i] for i in range(8)]
         total = gm[side, 10] * nodes[face]
@@ -392,7 +421,7 @@
     residual = finish(1, summed, rhs_copies)
     update = inverse * residual * (1.0 / centre)
     u = update
-    f, face_two = begin(2, rhs_ref[...] - operator(u))
+    f, face_two = begin_outside_in(2, u)
     ghosts = ghost_copies()
     for ghost in ghosts:
         ghost.start()
@@ -526,7 +555,7 @@
     f = jnp.concatenate([f[:1] + outer[:1], f[1:15], f[15:] + outer[1:]], axis=0)
     update = inv_ref[...] * f * (1.0 / centre)
     u = u + update
-    f, face_four = begin(4, rhs_ref[...] - operator(u))
+    f, face_four = begin_outside_in(4, u)
     residual = finish(4, f, face_four)
     update = (second_weight * first_weight) * update + (
         (2.0 * second_weight / half_width) * inv_ref[...]

time: 37.5 us -> 37 us (0.987)
  Pallas kernels: 34.6 us -> 34.1 us
    pallas_call x1, Pallas kernels: 34.6 us -> 34.1 us  [local(): pl.pallas_call(functools.partial(kernel, nw, nd, deriv), out_shape=(jax.S...]
where the time goes in v4:
time: 37 us; the launch traced here: 36.9 us
  Pallas kernels  34.1 us (92%)
  local copies, waits for them, and re-layouts  2.13 us (6%)
  between operations  0.65 us (2%)
    pallas_call x1, Pallas kernels, local(): pl.pallas_call(functools.partial(kernel, nw, nd, deriv), out_shape=(jax.S...  34.1 us
    unnamed x4, local copies, waits for them, and re-layouts  2.13 us

profile of v4, /device:TPU:0, one launch (start us, length us, event | category | flops | bytes accessed | tf_op | source)
XLA Modules:
  0.0 36.9 jit_solution(13448870635999651112)
XLA Ops:
  0.6 34.1 %shard_map.140 = (f32[16,16,128]{2,1,0:T(8,128)}, f32[1,2,32]{2,1,0:T(2,128)}) custom-call(f32[16,16,128]{2,1,0:T(8,128)} %refs_0_.1, f32[3,16,16,128]{3,2,1,0:T(8,128)} %refs_1_.1, f32[16,16,128]{2,1,0:T(8,128)} %refs_2_.1, s32[1,2,4,8]{3,2,1,0:T(4,128)} %refs_3_.1, s32[1,2,4]{2,1,0:T(2,128)} %refs_4_.1, f32[1,2,4,512]{3,2,1,0:T(4,128)} %refs_5_.1, ...), custom_call_target="tpu_custom_call" | custom-call | tf_op jit(solution)/shard_map/pallas_call | solution.py:580
  34.7 0.0 copy-start
  34.7 1.6 %copy.17 = f32[16,16,128]{2,1,0:T(8,128)} copy(f32[16,16,128]{2,1,0:T(8,128)} %get-tuple-element.4) | data formatting | bytes 262144
  36.3 0.0 copy-done
  36.3 0.6 %copy.18 = f32[1,2,32]{2,1,0:T(2,128)} copy(f32[1,2,32]{2,1,0:T(2,128)S(1)} %copy-done) | data formatting | bytes 512
Async XLA Ops:
  34.7 1.6 %copy-start = (f32[1,2,32]{2,1,0:T(2,128)S(1)}, f32[1,2,32]{2,1,0:T(2,128)}, u32[]{:S(2)}) copy-start(f32[1,2,32]{2,1,0:T(2,128)} %get-tuple-element.5) | copy-start | bytes 772
